TPU v7x, 128 devices: a whole 4x4x4 slice. The times are simulated.
128 devices in a mesh: seq: 64 (over z, x, y_lo, core), tp: 2 (over y_hi).
Axes of the slice: x: 4, y: 4 (y_hi: 2, y_lo: 2; y = y_hi * 2 + y_lo), z: 4, core: 2. Of those that a mesh axis runs over, the one named last changes fastest.
Arguments:
- latent: bfloat16 [64, 512, 1152], P('seq', 'tp'), may hold values from -6 to 6
- probe: bfloat16 [64, 512, 1152], P('seq', 'tp'), may hold values from -6 to 6
- adjoint: bfloat16 [64, 512, 1152], P('seq', 'tp'), may hold values from -6 to 6
- spatial_qkv: bfloat16 [1152, 3, 1152], P(None, None, 'tp'), may hold values from -0.1875 to 0.1875
- spatial_proj: bfloat16 [1152, 1152], P('tp'), may hold values from -0.75 to 0.75
- temporal_qkv: bfloat16 [1152, 3, 1152], P(None, None, 'tp'), may hold values from -0.1875 to 0.1875
- temporal_proj: bfloat16 [1152, 1152], P('tp'), may hold values from -0.75 to 0.75
Outputs:
- new_latent: bfloat16 [64, 512, 1152], P('seq', 'tp')
- new_adjoint: float32 [64, 512, 1152], P('seq', 'tp')
- trace_terms: float32 [64, 512], P('seq', 'tp')
All inputs are finite; a program needn't handle non-finite values.
Results may differ from a plain program's by a relative error of at most 0.025.
Values may be sent and summed in bfloat16 or wider, within the bound.
A program may use at most 192 MiB of HBM per device.

v0:
```python
import jax
import jax.numpy as jnp
from jax import lax
from jax.sharding import PartitionSpec as P

HEAD = 72


epsilon = 1e-06
step_size = 0.5


def contract(form, left, right):
    return jnp.einsum(form, left, right, preferred_element_type=jnp.float32)


def norm_stats(values):
    widened = values.astype(jnp.float32)
    centred = widened - jnp.mean(widened, axis=-1, keepdims=True)
    inverse = lax.rsqrt(jnp.mean(centred * centred, axis=-1, keepdims=True) + epsilon)
    return (centred * inverse, inverse)


def norm_tangent(normed, inverse, tangent):
    widened = tangent.astype(jnp.float32)
    centred = widened - jnp.mean(widened, axis=-1, keepdims=True)
    return inverse * (centred - normed * jnp.mean(normed * centred, axis=-1, keepdims=True))


def norm_back(normed, inverse, gradient):
    return inverse * (
        gradient
        - jnp.mean(gradient, axis=-1, keepdims=True)
        - normed * jnp.mean(normed * gradient, axis=-1, keepdims=True)
    )


def project(hidden, w_qkv):
    lead_dim, second = (hidden.shape[0], hidden.shape[1])
    head_count = w_qkv.shape[2] // HEAD
    projected = contract("abd,dcn->cabn", hidden, w_qkv).astype(jnp.bfloat16)
    return projected.reshape(3, lead_dim, second, head_count, HEAD)


def attend(projected, rows_spec, keys_spec):
    scores = contract(
        rows_spec + "," + keys_spec + "->ghlm", projected[0], projected[1]
    ) * HEAD ** (-0.5)
    attention = jax.nn.softmax(scores, axis=-1)
    weights = attention.astype(jnp.bfloat16)
    mixed_rows = contract("ghlm," + keys_spec + "->" + rows_spec, weights, projected[2]).astype(
        jnp.bfloat16
    )
    return (attention, weights, mixed_rows)


def attend_tangent(projected, tangents, attention, weights, rows_spec, keys_spec):
    to_scores = rows_spec + "," + keys_spec + "->ghlm"
    to_rows = "ghlm," + keys_spec + "->" + rows_spec
    score_tangent = (
        contract(to_scores, tangents[0], projected[1])
        + contract(to_scores, projected[0], tangents[1])
    ) * HEAD ** (-0.5)
    prob_tangent = attention * (
        score_tangent - jnp.sum(attention * score_tangent, axis=-1, keepdims=True)
    )
    mixed_tangent = contract(to_rows, prob_tangent.astype(jnp.bfloat16), projected[2]) + contract(
        to_rows, weights, tangents[2]
    )
    return mixed_tangent.astype(jnp.bfloat16)


def attend_back(projected, attention, weights, grad_mixed, rows_spec, keys_spec):
    to_scores = rows_spec + "," + keys_spec + "->ghlm"
    to_rows = "ghlm," + keys_spec + "->" + rows_spec
    to_keys = "ghlm," + rows_spec + "->" + keys_spec
    grad_weights = contract(to_scores, grad_mixed, projected[2])
    grad_value = contract(to_keys, weights, grad_mixed).astype(jnp.bfloat16)
    grad_scores = (
        attention
        * (grad_weights - jnp.sum(attention * grad_weights, axis=-1, keepdims=True))
        * HEAD ** (-0.5)
    )
    grad_scores = grad_scores.astype(jnp.bfloat16)
    grad_query = contract(to_rows, grad_scores, projected[1]).astype(jnp.bfloat16)
    grad_key = contract(to_keys, grad_scores, projected[0]).astype(jnp.bfloat16)
    return jnp.stack([grad_query, grad_key, grad_value])


def out_proj(mixed_rows, w_proj):
    flat_rows = mixed_rows.reshape(mixed_rows.shape[0], mixed_rows.shape[1], -1)
    return contract("abn,nd->abd", flat_rows, w_proj)


def block_primal(values, w_qkv, w_proj, rows_spec, keys_spec):
    normed, inverse = norm_stats(values)
    projected = project(normed.astype(jnp.bfloat16), w_qkv)
    attention, weights, mixed_rows = attend(projected, rows_spec, keys_spec)
    return (out_proj(mixed_rows, w_proj), (normed, inverse, projected, attention, weights))


def block_tangent(stored, tangent, w_qkv, w_proj, rows_spec, keys_spec):
    normed, inverse, projected, attention, weights = stored
    hidden_tangent = norm_tangent(normed, inverse, tangent).astype(jnp.bfloat16)
    tangents = project(hidden_tangent, w_qkv)
    return out_proj(
        attend_tangent(projected, tangents, attention, weights, rows_spec, keys_spec), w_proj
    )


def block_back(stored, gradient, w_qkv, w_proj, rows_spec, keys_spec):
    normed, inverse, projected, attention, weights = stored
    grad_mixed = (
        contract("abd,nd->abn", gradient, w_proj).astype(jnp.bfloat16).reshape(projected.shape[1:])
    )
    grad_stack = attend_back(projected, attention, weights, grad_mixed, rows_spec, keys_spec)
    flat_grads = grad_stack.reshape(3, grad_stack.shape[1], grad_stack.shape[2], -1)
    return contract("cabn,dcn->abd", flat_grads, w_qkv)


def local(latent, probe, adjoint, spatial_qkv, spatial_proj, temporal_qkv, temporal_proj):
    row_count = latent.shape[1]
    whole_latent, whole_probe, whole_adjoint = (
        lax.all_gather(latent, "tp", axis=1, tiled=True),
        lax.all_gather(probe, "tp", axis=1, tiled=True),
        lax.all_gather(adjoint, "tp", axis=1, tiled=True),
    )
    branch_part, stored_one = block_primal(whole_latent, spatial_qkv, spatial_proj, "glhe", "gmhe")
    dbranch_part = block_tangent(stored_one, whole_probe, spatial_qkv, spatial_proj, "glhe", "gmhe")
    branch_one, dbranch_one = lax.psum((branch_part, dbranch_part), "tp")
    inner_rows = (whole_latent.astype(jnp.float32) + branch_one).astype(jnp.bfloat16)
    inner_tangent = (whole_probe.astype(jnp.float32) + dbranch_one).astype(jnp.bfloat16)
    col_latent, col_tangent, col_adjoint = (
        lax.all_to_all(inner_rows, "seq", split_axis=1, concat_axis=0, tiled=True),
        lax.all_to_all(inner_tangent, "seq", split_axis=1, concat_axis=0, tiled=True),
        lax.all_to_all(whole_adjoint, "seq", split_axis=1, concat_axis=0, tiled=True),
    )
    branch_part, stored_two = block_primal(col_latent, temporal_qkv, temporal_proj, "lghe", "mghe")
    dbranch_part = block_tangent(
        stored_two, col_tangent, temporal_qkv, temporal_proj, "lghe", "mghe"
    )
    ghidden_part = block_back(stored_two, col_adjoint, temporal_qkv, temporal_proj, "lghe", "mghe")
    branch_two, dbranch_two, ghidden_two = lax.psum((branch_part, dbranch_part, ghidden_part), "tp")
    grad_two = norm_back(stored_two[0], stored_two[1], ghidden_two)
    returned = (
        lax.all_to_all(
            branch_two.astype(jnp.bfloat16), "seq", split_axis=0, concat_axis=1, tiled=True
        ),
        lax.all_to_all(
            dbranch_two.astype(jnp.bfloat16), "seq", split_axis=0, concat_axis=1, tiled=True
        ),
        lax.all_to_all(
            grad_two.astype(jnp.bfloat16), "seq", split_axis=0, concat_axis=1, tiled=True
        ),
    )
    grads_one = (whole_adjoint.astype(jnp.float32) + returned[2].astype(jnp.float32)).astype(
        jnp.bfloat16
    )
    ghidden_one = lax.psum(
        block_back(stored_one, grads_one, spatial_qkv, spatial_proj, "glhe", "gmhe"), "tp"
    )
    grad_one = norm_back(stored_one[0], stored_one[1], ghidden_one)
    offset = lax.axis_index("tp") * row_count

    def own_rows(values):
        return lax.dynamic_slice_in_dim(values, offset, row_count, 1)

    branch_one = own_rows(branch_one)
    dbranch_one = own_rows(dbranch_one)
    grad_one = own_rows(grad_one)
    branch_two = own_rows(returned[0])
    dbranch_two = own_rows(returned[1])
    grad_two = own_rows(returned[2])
    velocity = branch_one + branch_two.astype(jnp.float32)
    new_latent = (latent.astype(jnp.float32) + step_size * velocity).astype(jnp.bfloat16)
    trace_terms = jnp.mean(
        probe.astype(jnp.float32) * (dbranch_one + dbranch_two.astype(jnp.float32)), axis=-1
    )
    new_adjoint = adjoint.astype(jnp.float32) - step_size * (
        grad_one + grad_two.astype(jnp.float32)
    )
    return (new_latent, new_adjoint, trace_terms)


def solution(mesh):
    in_specs = (
        P("seq", "tp", None),
        P("seq", "tp", None),
        P("seq", "tp", None),
        P(None, None, "tp"),
        P("tp", None),
        P(None, None, "tp"),
        P("tp", None),
    )
    out_specs = (P("seq", "tp", None), P("seq", "tp", None), P("seq", "tp"))
    return jax.shard_map(local, mesh=mesh, in_specs=in_specs, out_specs=out_specs, check_vma=False)
```

profile of v0, /device:TPU:1, one launch (start us, length us, event | category | flops | bytes accessed | tf_op | source)
XLA Modules:
  0.0 884.5 jit_solution(8332427586001033414)
XLA Ops:
  8.7 31.0 %all-gather.4.cloned.1.call-done = bf16[1,512,1152]{2,1,0:T(8,128)(2,1)} async-done(((bf16[1,256,1152]{2,1,0:T(8,128)(2,1)}), bf16[1,512,1152]{2,1,0:T(8,128)(2,1)}) %all-gather.4.cloned.1.call-update) | async-done | bytes 1179664 | tf_op jit(solution)/shard_map/all_gather | solution.py:124
  49.1 7.5 fusion.182
  72.7 10.2 %reduce.19 = bf16[512,1152]{1,0:T(8,128)(2,1)} reduce(bf16[512,1,1152]{2,1,0:T(2,128)(2,1)} %bitcast.236, bf16[]{:T(256)} %broadcast.200), dimensions={1}, to_apply=%bitcast.234.reduce_sub_computation | reduce | bytes 2359298
  86.4 8.3 all-to-all-start.2
  94.6 64.2 %all-reduce.7.cloned.1.call-done = f32[1,512,1152]{2,1,0:T(8,128)} async-done(((f32[1,512,1152]{2,1,0:T(8,128)}), f32[1,512,1152]{2,1,0:T(8,128)}) %all-reduce.7.cloned.1.call-update) | async-done | bytes 2359312 | tf_op jit(solution)/shard_map/psum | solution.py:130
  164.0 9.8 %reduce.20 = bf16[512,1152]{1,0:T(8,128)(2,1)} reduce(bf16[512,1,1152]{2,1,0:T(2,128)(2,1)} %bitcast.238, bf16[]{:T(256)} %broadcast.200), dimensions={1}, to_apply=%bitcast.235.reduce_sub_computation | reduce | bytes 2359298
  177.4 8.3 all-to-all-start
  185.7 7.8 reshape.380
  198.7 6.3 all-to-all-done
  205.1 7.9 reshape.378
  226.9 5.8 convert_bitcast_fusion.1
  246.8 5.5 fusion.183
  252.4 6.2 fusion.76
  258.6 6.4 fusion.73
  278.3 7.1 fusion.25
  285.4 73.4 %all-reduce.9.cloned.1.call-done = f32[64,8,1152]{2,1,0:T(8,128)} async-done(((f32[64,8,1152]{2,1,0:T(8,128)}), f32[64,8,1152]{2,1,0:T(8,128)}) %all-reduce.9.cloned.1.call-update) | async-done | bytes 2359312 | tf_op jit(solution)/shard_map/psum | solution.py:143
  364.2 8.3 all-to-all-start.3
  373.1 18.8 %all-to-all-done.3 = bf16[64,8,1152]{2,1,0:T(8,128)(2,1)} async-done(((bf16[64,8,1152]{2,1,0:T(8,128)(2,1)}), bf16[64,8,1152]{2,1,0:T(8,128)(2,1)}, u32[]{:S(2)}, u32[]{:S(2)}) %all-to-all-start.3) | async-done | bytes 1179680 | tf_op jit(solution)/shard_map/all_to_all | solution.py:152
  394.5 5.7 convolution_convert_fusion.3
  404.7 15.0 %fusion.86 = bf16[8,72,512]{2,1,0:T(8,128)(2,1)} fusion(bf16[512,8,72]{0,2,1:T(8,128)(2,1)} %bitcast.244, f32[8,512,512]{1,2,0:T(8,128)} %fusion.188, f32[8,512,512]{1,2,0:T(8,128)} %get-tuple-element.24, f32[8,512]{1,0:T(8,128)S(1)} %copy-done.43), kind=kOutput, calls=%fused_computation.100 | convolution fusion | flops 316969472 | bytes 17973248 | tf_op jit(solution)/shard_map/ghlm,gmhe->glhe/dot_general | solution.py:14
  419.7 14.5 %fusion.89 = bf16[8,72,512]{2,1,0:T(8,128)(2,1)} fusion(bf16[512,8,72]{0,2,1:T(8,128)(2,1)} %bitcast.254, f32[8,512,512]{1,2,0:T(8,128)} %fusion.188, f32[8,512,512]{1,2,0:T(8,128)} %get-tuple-element.24, f32[8,512]{1,0:T(8,128)S(1)} %copy-done.43), kind=kOutput, calls=%fused_computation.101 | convolution fusion | flops 316969472 | bytes 17973248 | tf_op jit(solution)/shard_map/ghlm,glhe->gmhe/dot_general | solution.py:14
  434.3 6.7 convolution_bitcast_fusion.1
  443.0 71.4 %all-reduce.11.cloned.1.call-done = f32[1,512,1152]{2,1,0:T(8,128)} async-done(((f32[1,512,1152]{2,1,0:T(8,128)}), f32[1,512,1152]{2,1,0:T(8,128)}) %all-reduce.11.cloned.1.call-update) | async-done | bytes 2359312 | tf_op jit(solution)/shard_map/psum | solution.py:159
  537.5 76.3 %all-reduce.13.cloned.1.call-done = f32[1,512,1152]{2,1,0:T(8,128)} async-done(((f32[1,512,1152]{2,1,0:T(8,128)}), f32[1,512,1152]{2,1,0:T(8,128)}) %all-reduce.13.cloned.1.call-update) | async-done | bytes 2359312 | tf_op jit(solution)/shard_map/psum | solution.py:130
  618.8 8.8 reduce.21
  629.1 8.1 all-to-all-start.4
  646.6 10.1 %all-to-all-done.4 = bf16[64,2,4608]{2,1,0:T(2,128)(2,1)S(1)} async-done(((bf16[64,2,4608]{2,1,0:T(2,128)(2,1)}), bf16[64,2,4608]{2,1,0:T(2,128)(2,1)S(1)}, u32[]{:S(2)}, u32[]{:S(2)}) %all-to-all-start.4) | async-done | bytes 1179680 | tf_op jit(solution)/shard_map/all_to_all | solution.py:135
  668.3 9.2 %multiply_reduce_fusion.3 = f32[512]{0:T(512)S(1)} fusion(f32[512]{0:T(512)S(1)} %broadcast_multiply_fusion.3, f32[512]{0:T(512)S(1)} %copy-done.31, f32[512]{0:T(512)S(1)} %copy-done.29, bf16[512,1,1152]{2,1,0:T(2,128)(2,1)S(1)} %copy-done.3, bf16[512,1,1152]{2,1,0:T(2,128)(2,1)S(1)} %copy-done.2), kind=kLoop, calls=%fused_computation.51 | loop fusion | flops 4128256 | bytes 2367488 | tf_op jit(solution)/shard_map/reduce_sum | solution.py:27
  677.7 6.7 convert_bitcast_fusion
  709.1 113.5 %all-reduce.14 = (bf16[64,8,1152]{2,1,0:T(8,128)(2,1)}, bf16[64,8,1152]{2,1,0:T(8,128)(2,1)}) all-reduce(f32[64,8,1152]{2,1,0:T(8,128)} %fusion.83, f32[64,8,1152]{2,1,0:T(8,128)} %fusion.80), channel_id=1, replica_groups=mesh['seq'=64,'tp'=2] {'tp'}, use_global_device_ids=true, to_apply=%region_9.0 | all-reduce | flops 1179648 | bytes 7077888 | tf_op jit(solution)/shard_map/psum | solution.py:143
  822.6 25.8 %all_to_all.66 = bf16[64,8,1152]{2,1,0:T(8,128)(2,1)S(1)} all-to-all(bf16[64,8,1152]{2,1,0:T(8,128)(2,1)} %get-tuple-element.8), channel_id=1, replica_groups=mesh['seq'=64,'tp'=2] {'seq'}, dimensions={0} | all-to-all | bytes 2359296 | tf_op jit(solution)/shard_map/all_to_all | solution.py:146
  857.2 16.1 %all-to-all-done.5 = bf16[64,8,1152]{2,1,0:T(8,128)(2,1)} async-done(((bf16[64,8,1152]{2,1,0:T(8,128)(2,1)}), bf16[64,8,1152]{2,1,0:T(8,128)(2,1)}, u32[]{:S(2)}, u32[]{:S(2)}) %all-to-all-start.5) | async-done | bytes 1179680 | tf_op jit(solution)/shard_map/all_to_all | solution.py:149
  (195 shorter events, 188.4 us)
Async XLA Ops:
  7.2 53.7 %copy-start = (bf16[576,1152]{1,0:T(8,128)(2,1)S(1)}, bf16[576,1152]{1,0:T(8,128)(2,1)}, u32[]{:S(2)}) copy-start(bf16[576,1152]{1,0:T(8,128)(2,1)} %param.11) | copy-start | bytes 3981316
  7.2 32.6 %all-gather.4.cloned.1.call-start = ((), (), s32[]{:S(2)}) async-start(), calls=%async_computation.6 | async-start | bytes 1769472 | tf_op jit(solution)/shard_map/all_gather | solution.py:124
  7.9 59.7 %all-gather.6.cloned.1.call-start = ((), (), s32[]{:S(2)}) async-start(), calls=%async_computation.8 | async-start | bytes 1769472 | tf_op jit(solution)/shard_map/all_gather | solution.py:126
  8.7 150.2 %all-reduce.7.cloned.1.call-start = ((), (), s32[]{:S(2)}) async-start(), calls=%async_computation.7 | async-start | bytes 4718592 | tf_op jit(solution)/shard_map/psum | solution.py:130
  41.3 6.5 copy-start.32
  49.1 7.5 copy-start.14
  86.4 91.0 %all-to-all-start.2 = ((bf16[64,2,4608]{2,1,0:T(2,128)(2,1)}), bf16[64,2,4608]{2,1,0:T(2,128)(2,1)}, u32[]{:S(2)}, u32[]{:S(2)}) async-start(bf16[64,2,4608]{2,1,0:T(2,128)(2,1)} %reshape.379), calls=%async_computation.2 | async-start | bytes 2359296 | tf_op jit(solution)/shard_map/all_to_all | solution.py:136
  177.4 27.7 %all-to-all-start = ((bf16[64,2,4608]{2,1,0:T(2,128)(2,1)}), bf16[64,2,4608]{2,1,0:T(2,128)(2,1)}, u32[]{:S(2)}, u32[]{:S(2)}) async-start(bf16[64,2,4608]{2,1,0:T(2,128)(2,1)} %reshape.377), calls=%async_computation | async-start | bytes 2359296 | tf_op jit(solution)/shard_map/all_to_all | solution.py:134
  185.7 173.1 %all-reduce.9.cloned.1.call-start = ((), (), s32[]{:S(2)}) async-start(), calls=%async_computation.9 | async-start | bytes 4718592 | tf_op jit(solution)/shard_map/psum | solution.py:143
  217.3 9.5 %copy-start.28 = (f32[512]{0:T(512)}, f32[512]{0:T(512)S(1)}, u32[]{:S(2)}) copy-start(f32[512]{0:T(512)S(1)} %broadcast_multiply_fusion.8) | copy-start | bytes 6148
  236.6 10.2 %copy-start.9 = (bf16[64,8,8,72]{3,2,1,0:T(8,128)(2,1)}, bf16[64,8,8,72]{3,2,1,0:T(8,128)(2,1)S(1)}, u32[]{:S(2)}) copy-start(bf16[64,8,8,72]{3,2,1,0:T(8,128)(2,1)S(1)} %squeeze.12) | copy-start | bytes 1769476
  258.6 6.4 copy-start.13
  285.3 73.4 %copy-start.23 = (f32[64,8]{1,0:T(8,128)S(1)}, f32[64,8]{1,0:T(8,128)}, u32[]{:S(2)}) copy-start(f32[64,8]{1,0:T(8,128)} %copy-done.22) | copy-start | bytes 6148
  285.3 73.4 %copy-start.26 = (f32[64,8]{1,0:T(8,128)S(1)}, f32[64,8]{1,0:T(8,128)}, u32[]{:S(2)}) copy-start(f32[64,8]{1,0:T(8,128)} %copy-done.25) | copy-start | bytes 6148
  364.2 27.7 %all-to-all-start.3 = ((bf16[64,8,1152]{2,1,0:T(8,128)(2,1)}), bf16[64,8,1152]{2,1,0:T(8,128)(2,1)}, u32[]{:S(2)}, u32[]{:S(2)}) async-start(bf16[64,8,1152]{2,1,0:T(8,128)(2,1)} %multiply_convert_fusion.3), calls=%async_computation.3 | async-start | bytes 2359296 | tf_op jit(solution)/shard_map/all_to_all | solution.py:152
  372.5 69.0 %all-gather.8.cloned.1.call-start = ((), (), s32[]{:S(2)}) async-start(), calls=%async_computation.11 | async-start | bytes 1769472 | tf_op jit(solution)/shard_map/all_gather | solution.py:125
  373.1 21.4 %copy-start.43 = (f32[8,512]{1,0:T(8,128)S(1)}, f32[8,512]{1,0:T(8,128)}, u32[]{:S(2)}) copy-start(f32[8,512]{1,0:T(8,128)} %copy-done.42) | copy-start | bytes 49156
  373.1 141.3 %all-reduce.11.cloned.1.call-start = ((), (), s32[]{:S(2)}) async-start(), calls=%async_computation.10 | async-start | bytes 4718592 | tf_op jit(solution)/shard_map/psum | solution.py:159
  441.0 73.4 %copy-start.33 = (f32[512]{0:T(512)S(1)}, f32[512]{0:T(512)}, u32[]{:S(2)}) copy-start(f32[512]{0:T(512)} %copy-done.32) | copy-start | bytes 6148
  441.0 73.4 %copy-start.35 = (f32[512]{0:T(512)S(1)}, f32[512]{0:T(512)}, u32[]{:S(2)}) copy-start(f32[512]{0:T(512)} %copy-done.34) | copy-start | bytes 6148
  441.0 172.7 %all-reduce.13.cloned.1.call-start = ((), (), s32[]{:S(2)}) async-start(), calls=%async_computation.12 | async-start | bytes 4718592 | tf_op jit(solution)/shard_map/psum | solution.py:130
  514.4 10.0 %slice-start = ((s8[8388608]{0:T(1024)(128)(4,1)}), s8[4194304]{0:T(1024)(128)(4,1)S(1)}, s32[]{:S(2)}) async-start(s8[8388608]{0:T(1024)(128)(4,1)} %bitcast.264), calls=%async_computation.13 | async-start | bytes 8388608
  534.8 78.9 %copy-start.7 = (bf16[1,512,1152]{2,1,0:T(8,128)(2,1)S(1)}, bf16[1,512,1152]{2,1,0:T(8,128)(2,1)}, u32[]{:S(2)}) copy-start(bf16[1,512,1152]{2,1,0:T(8,128)(2,1)} %all-gather.8.cloned.1.call-done) | copy-start | bytes 3538948
  627.7 9.6 %copy-start.10 = (bf16[64,8,8,72]{3,2,1,0:T(8,128)(2,1)S(1)}, bf16[64,8,8,72]{3,2,1,0:T(8,128)(2,1)}, u32[]{:S(2)}) copy-start(bf16[64,8,8,72]{3,2,1,0:T(8,128)(2,1)} %copy-done.9) | copy-start | bytes 1769476
  629.1 27.6 %all-to-all-start.4 = ((bf16[64,2,4608]{2,1,0:T(2,128)(2,1)}), bf16[64,2,4608]{2,1,0:T(2,128)(2,1)S(1)}, u32[]{:S(2)}, u32[]{:S(2)}) async-start(bf16[64,2,4608]{2,1,0:T(2,128)(2,1)} %reshape.381), calls=%async_computation.4 | async-start | bytes 2359296 | tf_op jit(solution)/shard_map/all_to_all | solution.py:135
  668.2 9.4 %copy-start.24 = (f32[64,8]{1,0:T(8,128)S(1)}, f32[64,8]{1,0:T(8,128)}, u32[]{:S(2)}) copy-start(f32[64,8]{1,0:T(8,128)} %copy-done.22) | copy-start | bytes 6148
  668.3 9.4 %copy-start.27 = (f32[64,8]{1,0:T(8,128)S(1)}, f32[64,8]{1,0:T(8,128)}, u32[]{:S(2)}) copy-start(f32[64,8]{1,0:T(8,128)} %copy-done.25) | copy-start | bytes 6148
  822.6 31.2 %copy-start.36 = (f32[512]{0:T(512)S(1)}, f32[512]{0:T(512)}, u32[]{:S(2)}) copy-start(f32[512]{0:T(512)} %copy-done.34) | copy-start | bytes 6148
  822.6 31.2 %copy-start.37 = (f32[512]{0:T(512)S(1)}, f32[512]{0:T(512)}, u32[]{:S(2)}) copy-start(f32[512]{0:T(512)} %get-tuple-element.3) | copy-start | bytes 6148
  822.6 31.2 %copy-start.38 = (f32[512]{0:T(512)S(1)}, f32[512]{0:T(512)}, u32[]{:S(2)}) copy-start(f32[512]{0:T(512)} %get-tuple-element.4) | copy-start | bytes 6148
  822.6 31.4 %copy-start.17 = (bf16[1,256,1152]{2,1,0:T(8,128)(2,1)S(1)}, bf16[1,256,1152]{2,1,0:T(8,128)(2,1)}, u32[]{:S(2)}) copy-start(bf16[1,256,1152]{2,1,0:T(8,128)(2,1)} %param.9) | copy-start | bytes 1769476
  848.4 24.8 %all-to-all-start.5 = ((bf16[64,8,1152]{2,1,0:T(8,128)(2,1)}), bf16[64,8,1152]{2,1,0:T(8,128)(2,1)}, u32[]{:S(2)}, u32[]{:S(2)}) async-start(bf16[64,8,1152]{2,1,0:T(8,128)(2,1)} %get-tuple-element.9), calls=%async_computation.5 | async-start | bytes 2359296 | tf_op jit(solution)/shard_map/all_to_all | solution.py:149
  (26 other events, 109.1 us)
Sparse Core Ops, SparseCore 0:
  9.7 30.0 all-gather.3
  41.4 26.2 all-gather.5
  70.1 88.7 all-reduce.6
  285.5 73.2 all-reduce.8
  374.7 27.7 all-gather.7
  441.1 73.2 all-reduce.10
  537.6 76.0 all-reduce.12
where the time goes:
time: 895 us; the launch traced here: 884 us
  waiting for transfers between devices  374 us (42%)
  matrix products  154 us (17%)
  blocking collectives  139 us (16%)
  other arithmetic  85 us (9%)
  local copies, waits for them, and re-layouts  78 us (9%)
  starting transfers between devices  38.9 us (4%)
  between operations  15.2 us (2%)
    dot_general x30, matrix products, contract(): return jnp.einsum(form, left, right, preferred_element_type=jnp.float32)  141 us
    psum x2, waiting for transfers between devices, local(): branch_one, dbranch_one = lax.psum((branch_part, dbranch_part), 'tp')  140 us
    psum x1, blocking collectives, local(): lax.psum((branch_part, dbranch_part, ghidden_part), 'tp')  114 us
    psum x1, waiting for transfers between devices, local(): lax.psum((branch_part, dbranch_part, ghidden_part), 'tp')  73.4 us
    psum x1, waiting for transfers between devices, local(): lax.psum(block_back(stored_one, grads_one, spatial_qkv, spatial_proj, 'gl...  71.4 us
    all_gather x1, waiting for transfers between devices, local(): lax.all_gather(latent, 'tp', axis=1, tiled=True)  31 us
    unnamed x99, local copies, waits for them, and re-layouts  29.9 us
    unnamed x4, other arithmetic  28.9 us
  transfers between devices with their start and end apart: 12, of which 10 were waited for; matrix products, arithmetic and copies ran while one was open for 16% of the time, Pallas kernels for 0%

commit v1 on v0

v1 whole, which is shorter than its diff:
```python
import jax
import jax.numpy as jnp
from jax import lax
from jax.experimental import pallas as pl
from jax.experimental.pallas import tpu as pltpu
from jax.sharding import PartitionSpec as P

MESH = pl.DeviceIdType.MESH
BF = jnp.bfloat16
F32 = jnp.float32

epsilon = 1e-06
HEAD = 72
D = 1152
ROWS = 256
HALF = 576
PAD = 640
WIN = 256
GROUP = 64
SPAN = 4
SCALE = HEAD ** (-0.5)
EXP2 = SCALE * 1.4426950408889634


def nt(a, b):
    return lax.dot_general(a, b, (((1,), (1,)), ((), ())), preferred_element_type=F32)


def nn(a, b):
    return lax.dot_general(a, b, (((1,), (0,)), ((), ())), preferred_element_type=F32)


def tn(a, b):
    return lax.dot_general(a, b, (((0,), (0,)), ((), ())), preferred_element_type=F32)


def mean(v):
    return jnp.sum(v, axis=-1, keepdims=True) * (1.0 / D)


def norm_stats(x):
    centred = x - mean(x)
    inverse = lax.rsqrt(mean(centred * centred) + epsilon)
    return centred * inverse, inverse


def norm_tangent(normed, inverse, t):
    centred = t - mean(t)
    return inverse * (centred - normed * mean(normed * centred))


def norm_back(normed, inverse, g):
    return inverse * (g - mean(g) - normed * mean(normed * g))


def weight(ref, kind):
    return ref[kind].reshape(HALF, D)


def head_window(h):
    block = jnp.minimum(lax.div(h * 9, 16), 3)
    base = pl.multiple_of(block * 128, 128)
    lane = lax.broadcasted_iota(jnp.int32, (1, WIN), 1) + block * 128
    return pl.ds(base, WIN), (lane >= h * HEAD) & (lane < h * HEAD + HEAD)


def keep(mask, v):
    return jnp.where(mask, v, jnp.zeros_like(v))


def rank():
    s, t = lax.axis_index("seq"), lax.axis_index("tp")
    return s, t, lax.rem(s, 2)


def kernel(
    latent, probe, adjoint, wsq, wsp, wtq, wtp,
    o_latent, o_adjoint, o_trace,
    ws_own, ws_oth, wt_own, wt_oth,
    own_lat, own_prb, own_adj, x_lat, x_prb,
    hid, sq, sk, sv, sdq, sdk, sdv, probs,
    tq, tk, tv, tdq, tdk, tdv, tprobs,
    mix, gq, gk, gv, gsib_out, gsib_in, gh,
    m_inner, m_tan, m_adj, r_inner, r_tan, r_adj,
    m_g, m_u, m_d, r_g, r_u, r_d,
    v_out, v_in, tr_out, tr_in,
    l_sem, w_sem, swap_s, swap_r, sib_s, sib_r,
    gat_s, gat_r, fw_s, fw_r, a2a_s, a2a_r, gs_s, gs_r, end_s, end_r,
):
    s, t, c = rank()
    zx = lax.div(s, 4)
    z, x = lax.div(zx, 4), lax.rem(zx, 4)
    low = lax.rem(s, 4)
    stay = c == t
    swap_dev = (s - c + t, c)
    sib_dev = (s + 1 - 2 * c, t)
    y_dev = (s + 2 - 4 * lax.rem(lax.div(s, 2), 2), 1 - t)

    def remote(src, dst, ss, rs, dev):
        return pltpu.make_async_remote_copy(
            src_ref=src, dst_ref=dst, send_sem=ss, recv_sem=rs, device_id=dev, device_id_type=MESH
        )

    local = [
        pltpu.make_async_copy(wsq, ws_own.at[pl.ds(0, 3)], w_sem.at[0]),
        pltpu.make_async_copy(wsp, ws_own.at[3], w_sem.at[1]),
        pltpu.make_async_copy(latent.at[0], own_lat, l_sem.at[0]),
        pltpu.make_async_copy(probe.at[0], own_prb, l_sem.at[1]),
        pltpu.make_async_copy(adjoint.at[0], own_adj, l_sem.at[2]),
        pltpu.make_async_copy(wtq, wt_own.at[pl.ds(0, 3)], w_sem.at[2]),
        pltpu.make_async_copy(wtp, wt_own.at[3], w_sem.at[3]),
    ]
    for copy in local:
        copy.start()
    barrier = pltpu.get_barrier_semaphore()
    me = s * 2 + t

    def greet(k, carry):
        other = lax.rem(me + k, 2 * GROUP)
        pl.semaphore_signal(
            barrier, inc=1, device_id=(lax.div(other, 2), lax.rem(other, 2)), device_id_type=MESH
        )
        return carry

    lax.fori_loop(1, 2 * GROUP, greet, 0)
    for ref in (sq, sdq, tq, tdq):
        ref[:, :, pl.ds(HALF, PAD - HALF)] = jnp.zeros((2, ROWS, PAD - HALF), BF)
    for copy in local:
        copy.wait()
    pl.semaphore_wait(barrier, 2 * GROUP - 1)

    def parts(emit):
        for core, first, size in ((0, 0, 80), (1, 80, 64)):
            @pl.when(c == core)
            def _(core=core, first=first, size=size):
                emit(core, pl.ds(first, size), size)

    def line(ref, core, i, j, rows):
        if core == 0:
            return ref.at[i, :, rows, :]
        return ref.at[:, j, rows, :]

    def hop(core, k):
        if core == 0:
            return (lax.rem(z + k, 4) * 16 + x * 4 + low, t)
        return (z * 16 + lax.rem(x + k, 4) * 4 + low, t)

    def step(core, k):
        if core == 0:
            return (z * 16 + lax.rem(x + k, 4) * 4 + low, t)
        return (lax.rem(z + k, 4) * 16 + x * 4 + low, t)

    def gather_first(n, own, oth):
        def emit(core, rows, size):
            remote(
                own.at[z, x, rows, :], oth.at[z, x, rows, :],
                gat_s.at[n, 0], gat_r.at[n, 0], y_dev,
            ).start()
        parts(emit)

    def gather_second(n, own, oth):
        def emit(core, rows, size):
            remote(
                own.at[z, x, rows, :], oth.at[z, x, rows, :],
                gat_s.at[n, 0], gat_r.at[n, 0], y_dev,
            ).wait()
            for k in range(1, 4):
                remote(
                    oth.at[z, x, rows, :], oth.at[z, x, rows, :],
                    gat_s.at[n, k], gat_r.at[n, k], step(core, k),
                ).start()
        parts(emit)

    def gather_third(n, oth):
        def emit(core, rows, size):
            for k in range(1, 4):
                remote(
                    oth.at[z, x, rows, :], oth.at[z, x, rows, :],
                    gat_s.at[n, k], gat_r.at[n, k], step(core, k),
                ).wait()
            whole = line(oth, core, z, x, rows)
            for k in range(1, 4):
                remote(
                    whole, whole, gat_s.at[n, 3 + k], gat_r.at[n, 3 + k], hop(core, k)
                ).start()
            remote(whole, whole, fw_s.at[n, 0], fw_r.at[n, 0], sib_dev).start()
        parts(emit)

    def gather_fourth(n, oth):
        def emit(core, rows, size):
            for k in (1, 3, 2):
                came = line(oth, core, lax.rem(z - k + 4, 4), lax.rem(x - k + 4, 4), rows)
                remote(
                    came, came, gat_s.at[n, 3 + k], gat_r.at[n, 3 + k], hop(core, k)
                ).wait_recv()
                remote(came, came, fw_s.at[n, k], fw_r.at[n, k], sib_dev).start()
        parts(emit)

    def gather_last(n, oth):
        def emit(core, rows, size):
            whole = line(oth, core, z, x, rows)
            other_rows = pl.ds(80, 64) if core == 0 else pl.ds(0, 80)
            theirs = line(oth, 1 - core, z, x, other_rows)
            for k in range(4):
                remote(theirs, theirs, fw_s.at[n, k], fw_r.at[n, k], sib_dev).wait_recv()
                remote(whole, whole, fw_s.at[n, k], fw_r.at[n, k], sib_dev).wait_send()
            for k in range(1, 4):
                remote(
                    whole, whole, gat_s.at[n, 3 + k], gat_r.at[n, 3 + k], hop(core, k)
                ).wait_send()
        parts(emit)

    def exchange(n, src, dst, place, device, selfless):
        def send(k, carry):
            j = lax.rem(s + k, GROUP)
            remote(src.at[j], dst.at[place], a2a_s.at[n], a2a_r.at[n], device(j)).start()
            return carry

        if selfless is None:
            pltpu.make_async_copy(src.at[s], dst.at[s], a2a_r.at[n]).start()
        else:
            @pl.when(selfless)
            def _():
                pltpu.make_async_copy(src.at[s], dst.at[s], a2a_r.at[n]).start()

            @pl.when(jnp.logical_not(selfless))
            def _():
                send(0, 0)
        lax.fori_loop(1, GROUP, send, 0)

    def received(n, dst):
        remote(dst, dst, a2a_s.at[n], a2a_r.at[n], sib_dev).wait_recv()

    def sent(n, src, selfless):
        some = src.at[pl.ds(0, GROUP - 1)]
        remote(some, some, a2a_s.at[n], a2a_r.at[n], sib_dev).wait_send()
        if selfless is not None:
            @pl.when(jnp.logical_not(selfless))
            def _():
                one = src.at[0]
                remote(one, one, a2a_s.at[n], a2a_r.at[n], sib_dev).wait_send()

    def to_sibling(half, n, ref):
        return remote(
            ref.at[half, pl.ds(0, ROWS)], ref.at[half, pl.ds(ROWS, ROWS)],
            sib_s.at[half, n], sib_r.at[half, n], sib_dev,
        )

    frame = s - c + t

    gather_first(0, ws_own, ws_oth)

    @pl.when(jnp.logical_not(stay))
    def _():
        remote(own_lat, x_lat, swap_s.at[0], swap_r.at[0], swap_dev).start()
        remote(own_prb, x_prb, swap_s.at[1], swap_r.at[1], swap_dev).start()

    m_adj[...] = own_adj[...].reshape(GROUP, SPAN, D)
    gather_second(0, ws_own, ws_oth)

    def arrive(n, own, ref):
        @pl.when(stay)
        def _():
            ref[...] = own[...]

        @pl.when(jnp.logical_not(stay))
        def _():
            remote(own, ref, swap_s.at[n], swap_r.at[n], swap_dev).wait()

    arrive(0, own_lat, x_lat)
    hid[0] = norm_stats(x_lat[...].astype(F32))[0].astype(BF)

    def project(half, w, slot, q_ref, k_ref, v_ref, q_scale, exchange_rows):
        hidden = hid[slot]
        lanes = pl.ds(0, HALF)
        rows = pl.ds(0, ROWS)
        key = nt(hidden, weight(w, 1))
        k_ref[half, rows, lanes] = key.astype(BF)
        if exchange_rows is not None:
            to_sibling(half, exchange_rows, k_ref).start()
        v_ref[half, rows, lanes] = nt(hidden, weight(w, 2)).astype(BF)
        if exchange_rows is not None:
            to_sibling(half, exchange_rows + 1, v_ref).start()
        q_ref[half, rows, lanes] = nt(hidden, weight(w, 0)).astype(BF)

    def spatial_heads(half):
        mix[half] = jnp.zeros((ROWS, PAD), F32)

        def body(h, carry):
            win, mask = head_window(h)
            k = keep(mask, sk[half, :, win])
            scores = nt(sq[half, :, win], k)
            e = jnp.exp2((scores - jnp.max(scores, axis=-1, keepdims=True)) * EXP2)
            p = e * (1.0 / jnp.sum(e, axis=-1, keepdims=True))
            w = p.astype(BF)
            probs[half * 8 + h] = w
            mix[half, :, win] += nn(w, keep(mask, sv[half, :, win]))
            return carry

        lax.fori_loop(0, 8, body, 0)

    def tangent_heads(half, q_ref, k_ref, v_ref, dq_ref, dk_ref, dv_ref, p_ref):
        mix[half] = jnp.zeros((ROWS, PAD), F32)

        def body(h, carry):
            win, mask = head_window(h)
            k = keep(mask, k_ref[half, :, win])
            dk = keep(mask, dk_ref[half, :, win])
            ds = nt(dq_ref[half, :, win], k) + nt(q_ref[half, :, win], dk)
            w = p_ref[half * 8 + h]
            p = w.astype(F32)
            pd = p * (ds * SCALE)
            dp = (pd - p * jnp.sum(pd, axis=-1, keepdims=True)).astype(BF)
            out = nn(dp, keep(mask, v_ref[half, :, win]))
            out += nn(w, keep(mask, dv_ref[half, :, win]))
            mix[half, :, win] += out
            return carry

        lax.fori_loop(0, 8, body, 0)

    def out_proj(w_own, w_oth):
        lanes = pl.ds(0, HALF)
        first = nn(mix[0, :, lanes].astype(BF), weight(w_own, 3))
        return first + nn(mix[1, :, lanes].astype(BF), weight(w_oth, 3))

    project(0, ws_own, 0, sq, sk, sv, None, 0)
    gather_third(0, ws_oth)
    for n, ref in ((0, sk), (1, sv)):
        to_sibling(0, n, ref).wait()
    spatial_heads(0)
    gather_fourth(0, ws_oth)
    gather_last(0, ws_oth)
    project(1, ws_oth, 0, sq, sk, sv, None, 0)
    for n, ref in ((0, sk), (1, sv)):
        to_sibling(1, n, ref).wait()
    spatial_heads(1)
    inner = (x_lat[...].astype(F32) + out_proj(ws_own, ws_oth)).astype(BF)
    m_inner[...] = inner.reshape(GROUP, SPAN, D)
    exchange(0, m_inner, r_inner, frame, lambda j: (j, c), stay)
    exchange(1, m_adj, r_adj, s, lambda j: (j, t), None)
    gather_first(1, wt_own, wt_oth)

    arrive(1, own_prb, x_prb)
    normed, inverse = norm_stats(x_lat[...].astype(F32))
    hid[1] = norm_tangent(normed, inverse, x_prb[...].astype(F32)).astype(BF)
    project(0, ws_own, 1, sdq, sdk, sdv, None, 2)
    project(1, ws_oth, 1, sdq, sdk, sdv, None, 2)
    gather_second(1, wt_own, wt_oth)
    for half in range(2):
        for n, ref in ((2, sdk), (3, sdv)):
            to_sibling(half, n, ref).wait()
        tangent_heads(half, sq, sk, sv, sdq, sdk, sdv, probs)
    gather_third(1, wt_oth)
    moved = out_proj(ws_own, ws_oth)
    tangent = x_prb[...].astype(F32)
    tr_out[...] = jnp.broadcast_to(mean(tangent * moved), (ROWS, 128))
    m_tan[...] = (tangent + moved).astype(BF).reshape(GROUP, SPAN, D)
    exchange(2, m_tan, r_tan, frame, lambda j: (j, c), stay)

    row = lax.broadcasted_iota(jnp.int32, (ROWS, ROWS), 0)
    col = lax.broadcasted_iota(jnp.int32, (ROWS, ROWS), 1)
    same = lax.rem(row, SPAN) == lax.rem(col, SPAN)

    received(0, r_inner)
    x_inner = r_inner[...].reshape(ROWS, D).astype(F32)
    hid[0] = norm_stats(x_inner)[0].astype(BF)
    received(1, r_adj)

    def back_lanes(half, w, g):
        gm = nt(g, weight(w, 3)).astype(BF)
        sdq[half, :, pl.ds(0, HALF)] = gm

    def temporal_heads(half):
        mix[half] = jnp.zeros((ROWS, PAD), F32)
        gq[...] = jnp.zeros(gq.shape, F32)
        gk[...] = jnp.zeros(gk.shape, F32)
        gv[...] = jnp.zeros(gv.shape, F32)

        def body(h, carry):
            win, mask = head_window(h)
            q = tq[half, :, win]
            k = keep(mask, tk[half, :, win])
            v = keep(mask, tv[half, :, win])
            g = sdq[half, :, win]
            scores = jnp.where(same, nt(q, k), -1e30)
            e = jnp.exp2((scores - jnp.max(scores, axis=-1, keepdims=True)) * EXP2)
            p = e * (1.0 / jnp.sum(e, axis=-1, keepdims=True))
            w = p.astype(BF)
            tprobs[half * 8 + h] = w
            mix[half, :, win] += nn(w, v)
            gw = nt(g, v)
            pg = p * (gw * SCALE)
            gs = (pg - p * jnp.sum(pg, axis=-1, keepdims=True)).astype(BF)
            gq[:, win] += nn(gs, k)
            gk[pl.ds(0, ROWS), win] += tn(gs, keep(mask, q))
            gv[pl.ds(0, ROWS), win] += tn(w, keep(mask, g))
            return carry

        lax.fori_loop(0, 8, body, 0)

    def hidden_back(w):
        lanes = pl.ds(0, HALF)
        rows = pl.ds(0, ROWS)
        out = nn(gq[:, lanes].astype(BF), weight(w, 0))
        out += nn(gk[rows, lanes].astype(BF), weight(w, 1))
        return out + nn(gv[rows, lanes].astype(BF), weight(w, 2))

    g_two = r_adj[...].reshape(ROWS, D)
    project(0, wt_own, 0, tq, tk, tv, None, None)
    back_lanes(0, wt_own, g_two)
    temporal_heads(0)
    gh[...] = hidden_back(wt_own)
    gather_fourth(1, wt_oth)
    gather_last(1, wt_oth)
    project(1, wt_oth, 0, tq, tk, tv, None, None)
    back_lanes(1, wt_oth, r_adj[...].reshape(ROWS, D))
    temporal_heads(1)
    g_hidden = gh[...] + hidden_back(wt_oth)
    normed, inverse = norm_stats(r_inner[...].reshape(ROWS, D).astype(F32))
    grad_two = norm_back(normed, inverse, g_hidden).astype(BF).astype(F32)
    grads_one = (r_adj[...].reshape(ROWS, D).astype(F32) + grad_two).astype(BF)
    m_g[...] = grads_one.reshape(GROUP, SPAN, D)
    exchange(
        3, m_g, r_g, s, lambda f: (lax.div(f, 2) * 2 + t, lax.rem(f, 2)), stay
    )
    reached = r_inner[...].reshape(ROWS, D).astype(F32) + out_proj(wt_own, wt_oth)
    m_u[...] = reached.astype(BF).reshape(GROUP, SPAN, D)
    exchange(4, m_u, r_u, s, lambda f: (f, t), None)

    received(2, r_tan)
    normed, inverse = norm_stats(r_inner[...].reshape(ROWS, D).astype(F32))
    hid[1] = norm_tangent(normed, inverse, r_tan[...].reshape(ROWS, D).astype(F32)).astype(BF)
    project(0, wt_own, 1, tdq, tdk, tdv, None, None)
    project(1, wt_oth, 1, tdq, tdk, tdv, None, None)
    for half in range(2):
        tangent_heads(half, tq, tk, tv, tdq, tdk, tdv, tprobs)
    m_d[...] = out_proj(wt_own, wt_oth).astype(BF).reshape(GROUP, SPAN, D)
    exchange(5, m_d, r_d, s, lambda f: (f, t), None)

    received(3, r_g)

    def spatial_back(half):
        gq[...] = jnp.zeros(gq.shape, F32)
        gk[...] = jnp.zeros(gk.shape, F32)
        gv[...] = jnp.zeros(gv.shape, F32)

        def body(h, carry):
            win, mask = head_window(h)
            g = sdq[half, :, win]
            w = probs[half * 8 + h]
            p = w.astype(F32)
            gw = nt(g, keep(mask, sv[half, :, win]))
            pg = p * (gw * SCALE)
            gs = (pg - p * jnp.sum(pg, axis=-1, keepdims=True)).astype(BF)
            gq[:, win] += nn(gs, keep(mask, sk[half, :, win]))
            gk[:, win] += tn(gs, keep(mask, sq[half, :, win]))
            gv[:, win] += tn(w, keep(mask, g))
            return carry

        lax.fori_loop(0, 8, body, 0)

    def key_back(half):
        return remote(
            gsib_out.at[half], gsib_in.at[half], gs_s.at[half], gs_r.at[half], sib_dev
        )

    for half, w in ((0, ws_own), (1, ws_oth)):
        back_lanes(half, w, r_g[...].reshape(ROWS, D))
        spatial_back(half)
        gsib_out[half, 0] = gk[pl.ds(ROWS, ROWS), :].astype(BF)
        gsib_out[half, 1] = gv[pl.ds(ROWS, ROWS), :].astype(BF)
        key_back(half).start()
        lanes = pl.ds(0, HALF)
        part = nn(gq[:, lanes].astype(BF), weight(w, 0))
        if half == 0:
            gh[...] = part
        else:
            gh[...] += part
        key_back(half).wait()
        rows = pl.ds(0, ROWS)
        key = gk[rows, lanes] + gsib_in[half, 0, :, lanes].astype(F32)
        value = gv[rows, lanes] + gsib_in[half, 1, :, lanes].astype(F32)
        part = nn(key.astype(BF), weight(w, 1)) + nn(value.astype(BF), weight(w, 2))
        gh[...] += part
    normed, inverse = norm_stats(x_lat[...].astype(F32))
    grad_one = norm_back(normed, inverse, gh[...])
    v_out[...] = (grad_one + r_g[...].reshape(ROWS, D).astype(F32)).astype(BF)

    @pl.when(jnp.logical_not(stay))
    def _():
        remote(v_out, v_in, end_s.at[0], end_r.at[0], swap_dev).start()
        remote(tr_out, tr_in, end_s.at[1], end_r.at[1], swap_dev).start()

    @pl.when(stay)
    def _():
        v_in[...] = v_out[...]
        tr_in[...] = tr_out[...]

    received(4, r_u)
    o_latent[...] = (
        0.5 * (own_lat[...].astype(F32) + r_u[...].reshape(ROWS, D).astype(F32))
    ).astype(BF)
    received(5, r_d)
    extra = mean(own_prb[...].astype(F32) * r_d[...].reshape(ROWS, D).astype(F32))
    for n, ref, selfless in (
        (0, m_inner, stay), (1, m_adj, None), (2, m_tan, stay),
        (3, m_g, stay), (4, m_u, None), (5, m_d, None),
    ):
        sent(n, ref, selfless)

    @pl.when(jnp.logical_not(stay))
    def _():
        remote(v_out, v_in, end_s.at[0], end_r.at[0], swap_dev).wait()
        remote(tr_out, tr_in, end_s.at[1], end_r.at[1], swap_dev).wait()

    o_trace[...] = tr_in[...] + extra
    o_adjoint[...] = 1.5 * own_adj[...].astype(F32) - 0.5 * v_in[...].astype(F32)


def local(latent, probe, adjoint, spatial_qkv, spatial_proj, temporal_qkv, temporal_proj):
    def qkv(w):
        return jnp.transpose(w, (1, 2, 0)).reshape(3, 4, 144, D)

    def proj(w):
        return w.reshape(4, 144, D)

    dma = pltpu.SemaphoreType.DMA
    rows = pltpu.VMEM((ROWS, D), BF)
    weights = pltpu.VMEM((4, 4, 144, D), BF)
    one = pltpu.VMEM((2, ROWS, PAD), BF)
    two = pltpu.VMEM((2, 2 * ROWS, PAD), BF)
    message = pltpu.VMEM((GROUP, SPAN, D), BF)
    scratch = (
        [weights] * 4
        + [rows] * 5
        + [pltpu.VMEM((2, ROWS, D), BF)]
        + [one, two, two, one, two, two]
        + [pltpu.VMEM((16, ROWS, 2 * ROWS), BF)]
        + [one] * 6
        + [pltpu.VMEM((16, ROWS, ROWS), BF)]
        + [pltpu.VMEM((2, ROWS, PAD), F32), pltpu.VMEM((ROWS, PAD), F32)]
        + [pltpu.VMEM((2 * ROWS, PAD), F32)] * 2
        + [pltpu.VMEM((2, 2, ROWS, PAD), BF)] * 2
        + [pltpu.VMEM((ROWS, D), F32)]
        + [message] * 12
        + [rows] * 2
        + [pltpu.VMEM((ROWS, 128), F32)] * 2
        + [dma((3,)), dma((4,)), dma((2,)), dma((2,)), dma((2, 4)), dma((2, 4))]
        + [dma((2, 7)), dma((2, 7)), dma((2, 4)), dma((2, 4))]
        + [dma((6,)), dma((6,)), dma((2,)), dma((2,)), dma((2,)), dma((2,))]
    )
    new_latent, new_adjoint, trace = pl.pallas_call(
        kernel,
        out_shape=(
            jax.ShapeDtypeStruct((ROWS, D), BF),
            jax.ShapeDtypeStruct((ROWS, D), F32),
            jax.ShapeDtypeStruct((ROWS, 128), F32),
        ),
        in_specs=[pl.BlockSpec(memory_space=pl.ANY)] * 7,
        out_specs=[pl.BlockSpec(memory_space=pltpu.VMEM)] * 3,
        scratch_shapes=scratch,
        compiler_params=pltpu.CompilerParams(
            collective_id=0, has_side_effects=True, vmem_limit_bytes=63 << 20
        ),
    )(
        latent, probe, adjoint,
        qkv(spatial_qkv), proj(spatial_proj), qkv(temporal_qkv), proj(temporal_proj),
    )
    return new_latent[None], new_adjoint[None], trace[:, 0][None]


def solution(mesh):
    in_specs = (
        P("seq", "tp", None),
        P("seq", "tp", None),
        P("seq", "tp", None),
        P(None, None, "tp"),
        P("tp", None),
        P(None, None, "tp"),
        P("tp", None),
    )
    out_specs = (P("seq", "tp", None), P("seq", "tp", None), P("seq", "tp"))
    return jax.shard_map(local, mesh=mesh, in_specs=in_specs, out_specs=out_specs, check_vma=False)
```

time: 895 us -> 189 us (0.21); the launches traced: 884 us -> 189 us
  waiting for transfers between devices: 374 us -> 0 us
  Pallas kernels: 0 us -> 184 us
  matrix products: 154 us -> 0 us
  blocking collectives: 139 us -> 0 us
  other arithmetic: 85 us -> 0 us
  local copies, waits for them, and re-layouts: 78 us -> 4.62 us
  starting transfers between devices: 38.9 us -> 0 us
  between operations: 15.2 us -> 0.65 us
    psum x4 -> x0, waiting for transfers between devices: 285 us -> none  [the longest x2 140 us: local(): branch_one, dbranch_one = lax.psum((branch_part, dbranch_part), 'tp')]
    pallas_call x0 -> x1, Pallas kernels: none -> 184 us  [local(): pl.pallas_call(kernel, out_shape=(jax.ShapeDtypeStruct((ROWS, D), BF), ja...]
    dot_general x30 -> x0, matrix products: 141 us -> none  [contract(): return jnp.einsum(form, left, right, preferred_element_type=jnp.float32)]
    psum x1 -> x0, blocking collectives: 114 us -> none  [local(): lax.psum((branch_part, dbranch_part, ghidden_part), 'tp')]
    all_to_all x5 -> x0, waiting for transfers between devices: 51.2 us -> none  [the longest x1 18.8 us: local(): lax.all_to_all(grad_two.astype(jnp.bfloat16), 'seq', split_axis=0, concat...]
    all_to_all x5 -> x0, starting transfers between devices: 38.2 us -> none  [the longest x1 8.26 us: local(): lax.all_to_all(inner_rows, 'seq', split_axis=1, concat_axis=0, tiled=True)]
    reduce_sum x10 -> x0, other arithmetic: 37.6 us -> none  [the longest x1 9.17 us: norm_tangent(): jnp.mean(normed * centred, axis=-1, keepdims=True)]
    all_gather x3 -> x0, waiting for transfers between devices: 35.2 us -> none  [the longest x1 31 us: local(): lax.all_gather(latent, 'tp', axis=1, tiled=True)]
  transfers between devices with their start and end apart: 12 -> 0, of which waited for: 10 -> 0; matrix products, arithmetic and copies ran while one was open for 16% -> 0% of each run, Pallas kernels for 0% -> 0%
where the time goes in v1:
time: 189 us
  Pallas kernels  184 us (97%)
  local copies, waits for them, and re-layouts  4.62 us (2%)
    pallas_call x1, Pallas kernels, local(): pl.pallas_call(kernel, out_shape=(jax.ShapeDtypeStruct((ROWS, D), BF), ja...  184 us

profile of v1, /device:TPU:1, one launch (start us, length us, event | category | flops | bytes accessed | tf_op | source)
XLA Modules:
  0.0 189.1 jit_solution(4199409844889539796)
XLA Ops:
  0.6 183.8 %shard_map.94 = (bf16[256,1152]{1,0:T(8,128)(2,1)}, f32[256,1152]{1,0:T(8,128)}, f32[256,128]{1,0:T(8,128)}) custom-call(bf16[1,256,1152]{2,1,0:T(8,128)(2,1)} %latent.1, bf16[1,256,1152]{2,1,0:T(8,128)(2,1)} %probe.1, bf16[1,256,1152]{2,1,0:T(8,128)(2,1)} %adjoint.1, bf16[3,4,144,1152]{3,2,1,0:T(8,128)(2,1)} %bitcast.11, bf16[4,144,1152]{2,1,0:T(8,128)(2,1)} %bitcast.13, ...), custom_call_target="tpu_custom_call" | custom-call | tf_op jit(solution)/shard_map/pallas_call | solution.py:552
  184.4 0.0 copy-start
  184.4 1.7 slice_reduce_fusion
  186.1 1.9 %copy.12 = bf16[1,256,1152]{2,1,0:T(8,128)(2,1)} copy(bf16[1,256,1152]{2,1,0:T(8,128)(2,1)} %bitcast.16) | data formatting | bytes 1179648
  188.0 0.0 copy-done
  188.0 1.0 copy.13
Async XLA Ops:
  184.4 3.6 %copy-start = (f32[256,1152]{1,0:T(8,128)S(1)}, f32[256,1152]{1,0:T(8,128)}, u32[]{:S(2)}) copy-start(f32[256,1152]{1,0:T(8,128)} %get-tuple-element.7) | copy-start | bytes 3538948

commit v2 on v1

--- a/solution.py
+++ b/solution.py
@@ -75,17 +75,17 @@
 
 def kernel(
     latent, probe, adjoint, wsq, wsp, wtq, wtp,
-    o_latent, o_adjoint, o_trace,
+    o_reached, o_grads, o_trace,
     ws_own, ws_oth, wt_own, wt_oth,
     own_lat, own_prb, own_adj, x_lat, x_prb,
     hid, sq, sk, sv, sdq, sdk, sdv, probs,
-    tq, tk, tv, tdq, tdk, tdv, tprobs,
-    mix, gq, gk, gv, gsib_out, gsib_in, gh,
+    tq, tk, tv, tprobs,
+    mix, dmix, gq, gk, gv, gsib_out, gsib_in, gh,
     m_inner, m_tan, m_adj, r_inner, r_tan, r_adj,
     m_g, m_u, m_d, r_g, r_u, r_d,
     v_out, v_in, tr_out, tr_in,
     l_sem, w_sem, swap_s, swap_r, sib_s, sib_r,
-    gat_s, gat_r, fw_s, fw_r, a2a_s, a2a_r, gs_s, gs_r, end_s, end_r,
+    gat_s, gat_r, fw_s, fw_r, a2a_s, a2a_r, gs_s, gs_r, end_s, end_r, plane_sem, all_sem,
 ):
     s, t, c = rank()
     zx = lax.div(s, 4)
@@ -112,22 +112,24 @@
     ]
     for copy in local:
         copy.start()
+    y_line = [
+        (zx * 4 + lax.div(lax.rem(low * 2 + t + k, 8), 2), lax.rem(low * 2 + t + k, 2))
+        for k in range(1, 8)
+    ]
+    x_line = [(z * 16 + lax.rem(x + k, 4) * 4 + low, t) for k in range(1, 4)]
+    z_line = [(lax.rem(z + k, 4) * 16 + x * 4 + low, t) for k in range(1, 4)]
+
+    def greet(sem, devices):
+        for dev in devices:
+            pl.semaphore_signal(sem, inc=1, device_id=dev, device_id_type=MESH)
+
     barrier = pltpu.get_barrier_semaphore()
-    me = s * 2 + t
-
-    def greet(k, carry):
-        other = lax.rem(me + k, 2 * GROUP)
-        pl.semaphore_signal(
-            barrier, inc=1, device_id=(lax.div(other, 2), lax.rem(other, 2)), device_id_type=MESH
-        )
-        return carry
-
-    lax.fori_loop(1, 2 * GROUP, greet, 0)
-    for ref in (sq, sdq, tq, tdq):
+    greet(barrier, y_line + x_line + z_line)
+    for ref in (sq, sdq, tq):
         ref[:, :, pl.ds(HALF, PAD - HALF)] = jnp.zeros((2, ROWS, PAD - HALF), BF)
-    for copy in local:
+    for copy in local[:3]:
         copy.wait()
-    pl.semaphore_wait(barrier, 2 * GROUP - 1)
+    pl.semaphore_wait(barrier, 13)
 
     def parts(emit):
         for core, first, size in ((0, 0, 80), (1, 80, 64)):
@@ -135,10 +137,10 @@
             def _(core=core, first=first, size=size):
                 emit(core, pl.ds(first, size), size)
 
-    def line(ref, core, i, j, rows):
+    def line(ref, core, i, j, rows, some=pl.ds(0, 4)):
         if core == 0:
-            return ref.at[i, :, rows, :]
-        return ref.at[:, j, rows, :]
+            return ref.at[i, some, rows, :]
+        return ref.at[some, j, rows, :]
 
     def hop(core, k):
         if core == 0:
@@ -171,6 +173,8 @@
                 ).start()
         parts(emit)
 
+    halves = (pl.ds(0, 2), pl.ds(2, 2))
+
     def gather_third(n, oth):
         def emit(core, rows, size):
             for k in range(1, 4):
@@ -179,21 +183,30 @@
                     gat_s.at[n, k], gat_r.at[n, k], step(core, k),
                 ).wait()
             whole = line(oth, core, z, x, rows)
-            for k in range(1, 4):
-                remote(
-                    whole, whole, gat_s.at[n, 3 + k], gat_r.at[n, 3 + k], hop(core, k)
-                ).start()
+            for k, m in ((1, 4), (3, 6)):
+                remote(whole, whole, gat_s.at[n, m], gat_r.at[n, m], hop(core, k)).start()
             remote(whole, whole, fw_s.at[n, 0], fw_r.at[n, 0], sib_dev).start()
         parts(emit)
 
     def gather_fourth(n, oth):
         def emit(core, rows, size):
-            for k in (1, 3, 2):
-                came = line(oth, core, lax.rem(z - k + 4, 4), lax.rem(x - k + 4, 4), rows)
-                remote(
-                    came, came, gat_s.at[n, 3 + k], gat_r.at[n, 3 + k], hop(core, k)
-                ).wait_recv()
+            for k, m, some in ((1, 4, halves[0]), (3, 6, halves[1])):
+                i, j = lax.rem(z - k + 4, 4), lax.rem(x - k + 4, 4)
+                came = line(oth, core, i, j, rows)
+                part = line(oth, core, i, j, rows, some)
+                remote(came, came, gat_s.at[n, m], gat_r.at[n, m], hop(core, k)).wait_recv()
+                remote(part, part, gat_s.at[n, m + 1], gat_r.at[n, m + 1], hop(core, k)).start()
                 remote(came, came, fw_s.at[n, k], fw_r.at[n, k], sib_dev).start()
+        parts(emit)
+
+    def gather_fifth(n, oth):
+        def emit(core, rows, size):
+            i, j = lax.rem(z + 2, 4), lax.rem(x + 2, 4)
+            for k, m, some in ((1, 5, halves[0]), (3, 7, halves[1])):
+                part = line(oth, core, i, j, rows, some)
+                remote(part, part, gat_s.at[n, m], gat_r.at[n, m], hop(core, k)).wait_recv()
+            came = line(oth, core, i, j, rows)
+            remote(came, came, fw_s.at[n, 2], fw_r.at[n, 2], sib_dev).start()
         parts(emit)
 
     def gather_last(n, oth):
@@ -204,10 +217,9 @@
             for k in range(4):
                 remote(theirs, theirs, fw_s.at[n, k], fw_r.at[n, k], sib_dev).wait_recv()
                 remote(whole, whole, fw_s.at[n, k], fw_r.at[n, k], sib_dev).wait_send()
-            for k in range(1, 4):
-                remote(
-                    whole, whole, gat_s.at[n, 3 + k], gat_r.at[n, 3 + k], hop(core, k)
-                ).wait_send()
+            for m in range(4, 8):
+                gone = line(oth, core, z, x, rows, pl.ds(0, 4) if m % 2 == 0 else halves[0])
+                remote(gone, gone, gat_s.at[n, m], gat_r.at[n, m], hop(core, 1)).wait_send()
         parts(emit)
 
     def exchange(n, src, dst, place, device, selfless):
@@ -250,13 +262,19 @@
 
     gather_first(0, ws_own, ws_oth)
 
-    @pl.when(jnp.logical_not(stay))
-    def _():
-        remote(own_lat, x_lat, swap_s.at[0], swap_r.at[0], swap_dev).start()
-        remote(own_prb, x_prb, swap_s.at[1], swap_r.at[1], swap_dev).start()
-
+    def swap(n, own, ref):
+        @pl.when(jnp.logical_not(stay))
+        def _():
+            remote(own, ref, swap_s.at[n], swap_r.at[n], swap_dev).start()
+
+    swap(0, own_lat, x_lat)
+    greet(plane_sem, z_line)
+    for copy in local[3:]:
+        copy.wait()
     m_adj[...] = own_adj[...].reshape(GROUP, SPAN, D)
     gather_second(0, ws_own, ws_oth)
+    pl.semaphore_wait(plane_sem, 3)
+    greet(all_sem, y_line)
 
     def arrive(n, own, ref):
         @pl.when(stay)
@@ -268,6 +286,8 @@
             remote(own, ref, swap_s.at[n], swap_r.at[n], swap_dev).wait()
 
     arrive(0, own_lat, x_lat)
+    swap(1, own_prb, x_prb)
+    gather_third(0, ws_oth)
     hid[0] = norm_stats(x_lat[...].astype(F32))[0].astype(BF)
 
     def project(half, w, slot, q_ref, k_ref, v_ref, q_scale, exchange_rows):
@@ -283,8 +303,9 @@
             to_sibling(half, exchange_rows + 1, v_ref).start()
         q_ref[half, rows, lanes] = nt(hidden, weight(w, 0)).astype(BF)
 
-    def spatial_heads(half):
-        mix[half] = jnp.zeros((ROWS, PAD), F32)
+    def spatial_heads(half, first, last):
+        if first == 0:
+            mix[half] = jnp.zeros((ROWS, PAD), F32)
 
         def body(h, carry):
             win, mask = head_window(h)
@@ -297,61 +318,73 @@
             mix[half, :, win] += nn(w, keep(mask, sv[half, :, win]))
             return carry
 
-        lax.fori_loop(0, 8, body, 0)
-
-    def tangent_heads(half, q_ref, k_ref, v_ref, dq_ref, dk_ref, dv_ref, p_ref):
-        mix[half] = jnp.zeros((ROWS, PAD), F32)
+        lax.fori_loop(first, last, body, 0)
+
+    def tangent_heads(half, first, last, key_count, q_ref, k_ref, v_ref, dq_ref, dk_ref, dv_ref, p_ref):
+        keys = pl.ds(0, key_count)
+        if first == 0:
+            dmix[half] = jnp.zeros((ROWS, PAD), F32)
 
         def body(h, carry):
             win, mask = head_window(h)
-            k = keep(mask, k_ref[half, :, win])
-            dk = keep(mask, dk_ref[half, :, win])
+            k = keep(mask, k_ref[half, keys, win])
+            dk = keep(mask, dk_ref[half, keys, win])
             ds = nt(dq_ref[half, :, win], k) + nt(q_ref[half, :, win], dk)
             w = p_ref[half * 8 + h]
             p = w.astype(F32)
             pd = p * (ds * SCALE)
             dp = (pd - p * jnp.sum(pd, axis=-1, keepdims=True)).astype(BF)
-            out = nn(dp, keep(mask, v_ref[half, :, win]))
-            out += nn(w, keep(mask, dv_ref[half, :, win]))
-            mix[half, :, win] += out
+            out = nn(dp, keep(mask, v_ref[half, keys, win]))
+            out += nn(w, keep(mask, dv_ref[half, keys, win]))
+            dmix[half, :, win] += out
             return carry
 
-        lax.fori_loop(0, 8, body, 0)
-
-    def out_proj(w_own, w_oth):
+        lax.fori_loop(first, last, body, 0)
+
+    def out_proj(mixed, w_own, w_oth):
         lanes = pl.ds(0, HALF)
-        first = nn(mix[0, :, lanes].astype(BF), weight(w_own, 3))
-        return first + nn(mix[1, :, lanes].astype(BF), weight(w_oth, 3))
+        first = nn(mixed[0, :, lanes].astype(BF), weight(w_own, 3))
+        return first + nn(mixed[1, :, lanes].astype(BF), weight(w_oth, 3))
+
+    def siblings(half, pairs):
+        for n, ref in pairs:
+            to_sibling(half, n, ref).wait()
+
+    primal, moving = ((0, sk), (1, sv)), ((2, sdk), (3, sdv))
+    spatial = (2 * ROWS, sq, sk, sv, sdq, sdk, sdv, probs)
+    temporal = (ROWS, tq, tk, tv, sdq, sdk, sdv, tprobs)
 
     project(0, ws_own, 0, sq, sk, sv, None, 0)
-    gather_third(0, ws_oth)
-    for n, ref in ((0, sk), (1, sv)):
-        to_sibling(0, n, ref).wait()
-    spatial_heads(0)
+    siblings(0, primal)
+    spatial_heads(0, 0, 4)
     gather_fourth(0, ws_oth)
-    gather_last(0, ws_oth)
-    project(1, ws_oth, 0, sq, sk, sv, None, 0)
-    for n, ref in ((0, sk), (1, sv)):
-        to_sibling(1, n, ref).wait()
-    spatial_heads(1)
-    inner = (x_lat[...].astype(F32) + out_proj(ws_own, ws_oth)).astype(BF)
-    m_inner[...] = inner.reshape(GROUP, SPAN, D)
-    exchange(0, m_inner, r_inner, frame, lambda j: (j, c), stay)
-    exchange(1, m_adj, r_adj, s, lambda j: (j, t), None)
+    spatial_heads(0, 4, 8)
+    gather_fifth(0, ws_oth)
+
+    arrive(1, own_prb, x_prb)
     gather_first(1, wt_own, wt_oth)
-
-    arrive(1, own_prb, x_prb)
     normed, inverse = norm_stats(x_lat[...].astype(F32))
     hid[1] = norm_tangent(normed, inverse, x_prb[...].astype(F32)).astype(BF)
     project(0, ws_own, 1, sdq, sdk, sdv, None, 2)
+    siblings(0, moving)
+    tangent_heads(0, 0, 8, *spatial)
+    gather_last(0, ws_oth)
+    pl.semaphore_wait(all_sem, 7)
+    exchange(1, m_adj, r_adj, s, lambda j: (j, t), None)
+
+    project(1, ws_oth, 0, sq, sk, sv, None, 0)
+    gather_second(1, wt_own, wt_oth)
+    siblings(1, primal)
+    spatial_heads(1, 0, 8)
+    inner = (x_lat[...].astype(F32) + out_proj(mix, ws_own, ws_oth)).astype(BF)
+    m_inner[...] = inner.reshape(GROUP, SPAN, D)
+    exchange(0, m_inner, r_inner, frame, lambda j: (j, c), stay)
+    gather_third(1, wt_oth)
     project(1, ws_oth, 1, sdq, sdk, sdv, None, 2)
-    gather_second(1, wt_own, wt_oth)
-    for half in range(2):
-        for n, ref in ((2, sdk), (3, sdv)):
-            to_sibling(half, n, ref).wait()
-        tangent_heads(half, sq, sk, sv, sdq, sdk, sdv, probs)
-    gather_third(1, wt_oth)
-    moved = out_proj(ws_own, ws_oth)
+    siblings(1, moving)
+    tangent_heads(1, 0, 8, *spatial)
+    gather_fourth(1, wt_oth)
+    moved = out_proj(dmix, ws_own, ws_oth)
     tangent = x_prb[...].astype(F32)
     tr_out[...] = jnp.broadcast_to(mean(tangent * moved), (ROWS, 128))
     m_tan[...] = (tangent + moved).astype(BF).reshape(GROUP, SPAN, D)
@@ -409,8 +442,8 @@
     project(0, wt_own, 0, tq, tk, tv, None, None)
     back_lanes(0, wt_own, g_two)
     temporal_heads(0)
+    gather_fifth(1, wt_oth)
     gh[...] = hidden_back(wt_own)
-    gather_fourth(1, wt_oth)
     gather_last(1, wt_oth)
     project(1, wt_oth, 0, tq, tk, tv, None, None)
     back_lanes(1, wt_oth, r_adj[...].reshape(ROWS, D))
@@ -423,21 +456,21 @@
     exchange(
         3, m_g, r_g, s, lambda f: (lax.div(f, 2) * 2 + t, lax.rem(f, 2)), stay
     )
-    reached = r_inner[...].reshape(ROWS, D).astype(F32) + out_proj(wt_own, wt_oth)
+    reached = r_inner[...].reshape(ROWS, D).astype(F32) + out_proj(mix, wt_own, wt_oth)
     m_u[...] = reached.astype(BF).reshape(GROUP, SPAN, D)
-    exchange(4, m_u, r_u, s, lambda f: (f, t), None)
 
     received(2, r_tan)
     normed, inverse = norm_stats(r_inner[...].reshape(ROWS, D).astype(F32))
     hid[1] = norm_tangent(normed, inverse, r_tan[...].reshape(ROWS, D).astype(F32)).astype(BF)
-    project(0, wt_own, 1, tdq, tdk, tdv, None, None)
-    project(1, wt_oth, 1, tdq, tdk, tdv, None, None)
+    project(0, wt_own, 1, sdq, sdk, sdv, None, None)
+    project(1, wt_oth, 1, sdq, sdk, sdv, None, None)
     for half in range(2):
-        tangent_heads(half, tq, tk, tv, tdq, tdk, tdv, tprobs)
-    m_d[...] = out_proj(wt_own, wt_oth).astype(BF).reshape(GROUP, SPAN, D)
+        tangent_heads(half, 0, 8, *temporal)
+    m_d[...] = out_proj(dmix, wt_own, wt_oth).astype(BF).reshape(GROUP, SPAN, D)
+
+    received(3, r_g)
+    exchange(4, m_u, r_u, s, lambda f: (f, t), None)
     exchange(5, m_d, r_d, s, lambda f: (f, t), None)
-
-    received(3, r_g)
 
     def spatial_back(half):
         gq[...] = jnp.zeros(gq.shape, F32)
@@ -497,9 +530,7 @@
         tr_in[...] = tr_out[...]
 
     received(4, r_u)
-    o_latent[...] = (
-        0.5 * (own_lat[...].astype(F32) + r_u[...].reshape(ROWS, D).astype(F32))
-    ).astype(BF)
+    o_reached[...] = r_u[...].reshape(ROWS, D)
     received(5, r_d)
     extra = mean(own_prb[...].astype(F32) * r_d[...].reshape(ROWS, D).astype(F32))
     for n, ref, selfless in (
@@ -513,8 +544,8 @@
         remote(v_out, v_in, end_s.at[0], end_r.at[0], swap_dev).wait()
         remote(tr_out, tr_in, end_s.at[1], end_r.at[1], swap_dev).wait()
 
-    o_trace[...] = tr_in[...] + extra
-    o_adjoint[...] = 1.5 * own_adj[...].astype(F32) - 0.5 * v_in[...].astype(F32)
+    o_trace[...] = jnp.transpose(tr_in[...] + extra)[0:8]
+    o_grads[...] = v_in[...]
 
 
 def local(latent, probe, adjoint, spatial_qkv, spatial_proj, temporal_qkv, temporal_proj):
@@ -536,9 +567,10 @@
         + [pltpu.VMEM((2, ROWS, D), BF)]
         + [one, two, two, one, two, two]
         + [pltpu.VMEM((16, ROWS, 2 * ROWS), BF)]
-        + [one] * 6
+        + [one] * 3
         + [pltpu.VMEM((16, ROWS, ROWS), BF)]
-        + [pltpu.VMEM((2, ROWS, PAD), F32), pltpu.VMEM((ROWS, PAD), F32)]
+        + [pltpu.VMEM((2, ROWS, PAD), F32)] * 2
+        + [pltpu.VMEM((ROWS, PAD), F32)]
         + [pltpu.VMEM((2 * ROWS, PAD), F32)] * 2
         + [pltpu.VMEM((2, 2, ROWS, PAD), BF)] * 2
         + [pltpu.VMEM((ROWS, D), F32)]
@@ -546,15 +578,16 @@
         + [rows] * 2
         + [pltpu.VMEM((ROWS, 128), F32)] * 2
         + [dma((3,)), dma((4,)), dma((2,)), dma((2,)), dma((2, 4)), dma((2, 4))]
-        + [dma((2, 7)), dma((2, 7)), dma((2, 4)), dma((2, 4))]
+        + [dma((2, 8)), dma((2, 8)), dma((2, 4)), dma((2, 4))]
         + [dma((6,)), dma((6,)), dma((2,)), dma((2,)), dma((2,)), dma((2,))]
+        + [pltpu.SemaphoreType.REGULAR] * 2
     )
-    new_latent, new_adjoint, trace = pl.pallas_call(
+    reached, grads, trace = pl.pallas_call(
         kernel,
         out_shape=(
             jax.ShapeDtypeStruct((ROWS, D), BF),
-            jax.ShapeDtypeStruct((ROWS, D), F32),
-            jax.ShapeDtypeStruct((ROWS, 128), F32),
+            jax.ShapeDtypeStruct((ROWS, D), BF),
+            jax.ShapeDtypeStruct((8, ROWS), F32),
         ),
         in_specs=[pl.BlockSpec(memory_space=pl.ANY)] * 7,
         out_specs=[pl.BlockSpec(memory_space=pltpu.VMEM)] * 3,
@@ -566,7 +599,9 @@
         latent, probe, adjoint,
         qkv(spatial_qkv), proj(spatial_proj), qkv(temporal_qkv), proj(temporal_proj),
     )
-    return new_latent[None], new_adjoint[None], trace[:, 0][None]
+    new_latent = (0.5 * (latent.astype(F32) + reached[None].astype(F32))).astype(BF)
+    new_adjoint = 1.5 * adjoint.astype(F32) - 0.5 * grads[None].astype(F32)
+    return new_latent, new_adjoint, trace[0:1]
 
 
 def solution(mesh):

time: 189 us -> 169 us (0.89)
  Pallas kernels: 184 us -> 164 us
  local copies, waits for them, and re-layouts: 4.62 us -> 1.26 us
  other arithmetic: 0 us -> 2.99 us
    pallas_call x1, Pallas kernels: 184 us -> 164 us  [local(): pl.pallas_call(kernel, out_shape=(jax.ShapeDtypeStruct((ROWS, D), BF), ja...]
    convert_element_type x0 -> x1, other arithmetic: none -> 2.99 us  [local(): (0.5 * (latent.astype(F32) + reached[None].astype(F32))).astype(BF)]
    unnamed x4 -> x2, local copies, waits for them, and re-layouts: 2.94 us -> 0.01 us
where the time goes in v2:
time: 169 us
  Pallas kernels  164 us (97%)
  other arithmetic  2.99 us (2%)
    pallas_call x1, Pallas kernels, local(): pl.pallas_call(kernel, out_shape=(jax.ShapeDtypeStruct((ROWS, D), BF), ja...  164 us

profile of v2, /device:TPU:1, one launch (start us, length us, event | category | flops | bytes accessed | tf_op | source)
XLA Modules:
  0.0 169.2 jit_solution(12374468535409476711)
XLA Ops:
  0.6 0.0 copy-start
  0.6 164.3 %shard_map.94 = (bf16[256,1152]{1,0:T(8,128)(2,1)}, bf16[256,1152]{1,0:T(8,128)(2,1)}, f32[8,256]{1,0:T(8,128)}) custom-call(bf16[1,256,1152]{2,1,0:T(8,128)(2,1)} %latent.1, bf16[1,256,1152]{2,1,0:T(8,128)(2,1)} %probe.1, bf16[1,256,1152]{2,1,0:T(8,128)(2,1)} %adjoint.1, bf16[3,4,144,1152]{3,2,1,0:T(8,128)(2,1)} %bitcast.13, ...), custom_call_target="tpu_custom_call" | custom-call | tf_op jit(solution)/shard_map/pallas_call | solution.py:585
  164.9 1.3 slice.3
  166.2 0.0 copy-done
  166.2 3.0 %fusion.1 = (bf16[1,256,1152]{2,1,0:T(8,128)(2,1)}, f32[1,256,1152]{2,1,0:T(8,128)}) fusion(bf16[1,256,1152]{2,1,0:T(8,128)(2,1)S(1)} %copy-done, bf16[256,1152]{1,0:T(8,128)(2,1)} %get-tuple-element.6, bf16[256,1152]{1,0:T(8,128)(2,1)} %get-tuple-element.7, bf16[1,256,1152]{2,1,0:T(8,128)(2,1)} %adjoint.1), kind=kLoop, calls=%fused_computation.2 | loop fusion | flops 2949120 | bytes 4128768 | tf_op jit(solution)/shard_map/convert_element_type | solution.py:602
Async XLA Ops:
  0.6 165.6 %copy-start = (bf16[1,256,1152]{2,1,0:T(8,128)(2,1)S(1)}, bf16[1,256,1152]{2,1,0:T(8,128)(2,1)}, u32[]{:S(2)}) copy-start(bf16[1,256,1152]{2,1,0:T(8,128)(2,1)} %latent.1) | copy-start | bytes 1769476
